TPU v7x, 32 devices: a whole 2x2x4 slice. The times are simulated.
32 devices in a mesh: real: 2 (over x), tx: 16 (over z, y, core).
Axes of the slice: x: 2, y: 2, z: 4, core: 2. Of those that a mesh axis runs over, the one named last changes fastest.
Arguments:
- misfit_source: float32 [512, 2048], P(('real', 'tx')), parts along dimension 0, may hold values from -24 to 24
- storage: float32 [512, 2048], P(('real', 'tx')), parts along dimension 0, may hold values from 0.02 to 0.5
- conduct_x: float32 [512, 2048], P(('real', 'tx')), parts along dimension 0, may hold values from 0.2 to 5
- conduct_y: float32 [512, 2048], P(('real', 'tx')), parts along dimension 0, may hold values from 0.2 to 5
- well_row: int32 [640], P('tx'), may hold values from 0 to 15
- well_col: int32 [640], P('tx'), may hold values from 0 to 1920
- well_owner: int32 [640, 1], P('tx'), may hold values from 0 to 15
- well_slot: int32 [640], P('tx'), may hold values from 0 to 7
- connection: float32 [640, 128], P('tx'), may hold values from 0.1 to 2
Outputs:
- adjoint_head: float32 [512, 2048], P(('real', 'tx')), parts along dimension 0
- plan_grad: float32 [256, 128], P(('real', 'tx')), parts along dimension 0
There are 2 independent parts, one for each index of `real`. A program takes and returns all parts, laid end to end along the dimension named above; an argument that names none is the same for every part. Nothing has to cross between parts.
All inputs are finite; a program needn't handle non-finite values.
Results may differ from a plain program's by a relative error of at most 0.0001.
Values sent between devices are 32-bit elements; how exact they have to be, the bound alone decides.
A program may use at most 64 MiB of HBM per device.

v0:
```python
import jax
import jax.numpy as jnp
from jax import lax
from jax.sharding import PartitionSpec as P

BLK_DEV = 8
SCREEN = 128
LEVELS = 5
NU = 2
CSW = 16


omega_damp = 0.8


def padded_2(cells, sides, width):
    for axis, dim in sides:
        count = lax.axis_size(axis)
        ends = count - 1
        head = lax.slice_in_dim(cells, 0, width, axis=dim)
        tail = lax.slice_in_dim(cells, cells.shape[dim] - width, cells.shape[dim], axis=dim)
        cells = jnp.concatenate(
            [
                lax.ppermute(tail, axis, [(i, (i + 1) % count) for i in range(ends)]),
                cells,
                lax.ppermute(head, axis, [((i + 1) % count, i) for i in range(ends)]),
            ],
            axis=dim,
        )
    return cells


def passed_along(value, axis, steps):
    count = lax.axis_size(axis)
    leading, last = (max(0, -steps), min(count, count - steps))
    return lax.ppermute(value, axis, [(source, source + steps) for source in range(leading, last)])


def coarsen(storage, along_x, along_y):
    rows, cols = storage.shape
    coarse_store = storage.reshape(rows // 2, 2, cols // 2, 2).sum(axis=(1, 3))
    coarse_x = along_x[1::2].reshape(rows // 2, cols // 2, 2).sum(axis=2)
    coarse_y = (along_y[0::2] + along_y[1::2])[:, 1::2]
    return (coarse_store, coarse_x, coarse_y)


def operators(storage, along_x, below_x, along_y):
    left_y = jnp.pad(along_y[:, :-1], ((0, 0), (1, 0)))
    diagonal = storage + along_x + below_x + along_y + left_y
    return (storage, along_x, below_x, along_y, left_y, diagonal)


def apply_operator(field, padded, ops):
    storage, along_x, below_x, along_y, left_y, diagonal = ops
    upper = padded[2:]
    lower = padded[:-2]
    right_cell = jnp.pad(field[:, 1:], ((0, 0), (0, 1)))
    left_cell = jnp.pad(field[:, :-1], ((0, 0), (1, 0)))
    return (
        storage * field
        + along_x * (field - upper)
        + below_x * (field - lower)
        + along_y * (field - right_cell)
        + left_y * (field - left_cell)
    )


def residual_of(field, source, ops):
    padded = padded_2(field, (("tx", 0),), 1)
    return source - apply_operator(field, padded, ops)


def smooth(field, source, ops):
    return field + omega_damp * residual_of(field, source, ops) / ops[5]


def restrict(field):
    rows, cols = field.shape
    return field.reshape(rows // 2, 2, cols // 2, 2).sum(axis=(1, 3))


def prolong(field):
    rows, cols = field.shape
    return jnp.broadcast_to(field[:, None, :, None], (rows, 2, cols, 2)).reshape(rows * 2, cols * 2)


def coarsest_solve(source, ops):
    start_field = jnp.zeros(source.shape, jnp.float32)
    return lax.fori_loop(0, CSW, lambda index, value: smooth(value, source, ops), start_field)


def vcycle(source, hierarchy, depth):
    ops = hierarchy[depth]
    if depth == len(hierarchy) - 1:
        return coarsest_solve(source, ops)
    field = jnp.zeros(source.shape, jnp.float32)
    for sweep_index in range(NU):
        field = smooth(field, source, ops)
    coarse_source = restrict(residual_of(field, source, ops))
    field = field + prolong(vcycle(coarse_source, hierarchy, depth + 1))
    for sweep_index in range(NU):
        field = smooth(field, source, ops)
    return field


def shards(
    misfit_source,
    storage,
    conduct_x,
    conduct_y,
    well_row,
    well_col,
    well_owner,
    well_slot,
    connection,
):
    lower_row = passed_along(conduct_x[-1:], "tx", 1)
    hierarchy = []
    store_now, along_x, along_y = (storage, conduct_x, conduct_y)
    for depth_index in range(LEVELS):
        below_x = jnp.concatenate([lower_row, along_x[:-1]], axis=0)
        hierarchy.append(operators(store_now, along_x, below_x, along_y))
        if depth_index < LEVELS - 1:
            store_now, along_x, along_y = coarsen(store_now, along_x, along_y)
            lower_row = lower_row.reshape(1, lower_row.shape[1] // 2, 2).sum(axis=2)
    adjoint_head = vcycle(misfit_source, hierarchy, 0)
    picked = adjoint_head[well_row]
    window = jax.vmap(lambda line, start_col: lax.dynamic_slice_in_dim(line, start_col, SCREEN))(
        picked, well_col
    )
    terms = connection * window
    my_owner = lax.axis_index("tx")
    slot_ids = jnp.arange(BLK_DEV, dtype=jnp.int32)
    piece_terms = lax.all_gather(terms, "tx", axis=0, tiled=True)
    piece_owner = lax.all_gather(well_owner, "tx", axis=0, tiled=True)
    piece_slot = lax.all_gather(well_slot, "tx", axis=0, tiled=True)
    mine = piece_owner[:, 0] == my_owner
    one_hot = ((piece_slot[:, None] == slot_ids[None, :]) & mine[:, None]).astype(jnp.float32)
    plan_grad = lax.dot_general(
        one_hot,
        piece_terms,
        (((0,), (0,)), ((), ())),
        precision=lax.Precision.HIGHEST,
        preferred_element_type=jnp.float32,
    )
    return (adjoint_head, plan_grad)


def solution(mesh):
    return jax.shard_map(
        shards,
        mesh=mesh,
        in_specs=(
            P(("real", "tx"), None),
            P(("real", "tx"), None),
            P(("real", "tx"), None),
            P(("real", "tx"), None),
            P("tx"),
            P("tx"),
            P("tx", None),
            P("tx"),
            P("tx", None),
        ),
        out_specs=(P(("real", "tx"), None), P(("real", "tx"), None)),
        check_vma=False,
    )
```

profile of v0, /device:TPU:0, one launch (start us, length us, event | category | flops | bytes accessed | tf_op | source)
XLA Modules:
  0.0 455.0 jit_solution(325711224858799726)
XLA Ops:
  28.4 11.8 %all-reduce.57 = (s32[640]{0:T(1024)S(1)}, s32[640]{0:T(1024)S(1)}) all-reduce(s32[640]{0:T(1024)S(1)} %dynamic-update-slice.2, s32[640]{0:T(1024)S(1)} %bitcast_dynamic-update-slice_fusion), channel_id=1, replica_groups=mesh['real'=2,'tx'=16] {'tx'}, use_global_device_ids=true, to_apply=%add.55 | all-reduce | flops 1280 | bytes 10240
  41.4 10.5 %reshape.102 = f32[8,2,1024,2]{3,2,1,0:T(8,128)} reshape(f32[16,2048]{1,0:T(8,128)S(1)} %copy-done.3) | data formatting | bytes 262144 | tf_op jit(solution)/shard_map/reshape | solution.py:41
  80.1 10.5 %reshape.101 = f32[8,2,1024,2]{3,2,1,0:T(8,128)} reshape(f32[16,2048]{1,0:T(8,128)S(1)} %get-tuple-element.213) | data formatting | bytes 262144 | tf_op jit(solution)/shard_map/reshape | solution.py:79
  118.8 5.9 %collective-permute-start.18 = (f32[1,512]{1,0:T(1,128)S(1)}, f32[1,512]{1,0:T(1,128)S(1)}, u32[]{:S(2)}, u32[]{:S(2)}) collective-permute-start(f32[1,512]{1,0:T(1,128)S(1)} %get-tuple-element.253), channel_id=1, source_target_pairs={{0,1},{1,2},{2,3},{3,4},{4,5},{5,6},{6,7},{7,8},{8,9},{9,10},{10,1... | collective-permute-start | bytes 6152 | tf_op jit(solution)/shard_map/ppermute | solution.py:24
  146.8 124.1 %while.15 = (s32[]{:T(128)}, f32[1,128]{1,0:T(1,128)S(1)}, f32[1,128]{1,0:T(1,128)S(1)}, f32[1,128]{1,0:T(1,128)S(1)}, f32[1,128]{1,0:T(1,128)S(1)}, /*index=5*/...) while((s32[]{:T(128)}, f32[1,128]{1,0:T(1,128)S(1)}, ...), condition=%wide.region_22.23_spmd.clone, body=%wide.region_21.22_spmd.clone.sunk | while | flops 2435 | bytes 14000 | solution.py:89
  148.1 5.2 %collective-permute-start = (f32[1,128]{1,0:T(1,128)S(1)}, f32[1,128]{1,0:T(1,128)S(1)}, u32[]{:S(2)}, u32[]{:S(2)}) collective-permute-start(f32[1,128]{1,0:T(1,128)S(1)} %broadcast_select_fusion.2), channel_id=1, source_target_pairs={{0,1},{1,2},{2,3},{3,4},{4,5},{5,6},{6,7},{7,8},{8,9},{9,10},{10,1... | collective-permute-start | bytes 1544 | tf_op jit(solution)/shard_map/while/body/eval_jaxpr/ppermute | solution.py:24
  155.5 5.6 %collective-permute-start = (f32[1,128]{1,0:T(1,128)S(1)}, f32[1,128]{1,0:T(1,128)S(1)}, u32[]{:S(2)}, u32[]{:S(2)}) collective-permute-start(f32[1,128]{1,0:T(1,128)S(1)} %broadcast_select_fusion.2), channel_id=1, source_target_pairs={{0,1},{1,2},{2,3},{3,4},{4,5},{5,6},{6,7},{7,8},{8,9},{9,10},{10,1... | collective-permute-start | bytes 1544 | tf_op jit(solution)/shard_map/while/body/eval_jaxpr/ppermute | solution.py:24
  163.3 5.6 %collective-permute-start = (f32[1,128]{1,0:T(1,128)S(1)}, f32[1,128]{1,0:T(1,128)S(1)}, u32[]{:S(2)}, u32[]{:S(2)}) collective-permute-start(f32[1,128]{1,0:T(1,128)S(1)} %broadcast_select_fusion.2), channel_id=1, source_target_pairs={{0,1},{1,2},{2,3},{3,4},{4,5},{5,6},{6,7},{7,8},{8,9},{9,10},{10,1... | collective-permute-start | bytes 1544 | tf_op jit(solution)/shard_map/while/body/eval_jaxpr/ppermute | solution.py:24
  171.1 5.6 %collective-permute-start = (f32[1,128]{1,0:T(1,128)S(1)}, f32[1,128]{1,0:T(1,128)S(1)}, u32[]{:S(2)}, u32[]{:S(2)}) collective-permute-start(f32[1,128]{1,0:T(1,128)S(1)} %broadcast_select_fusion.2), channel_id=1, source_target_pairs={{0,1},{1,2},{2,3},{3,4},{4,5},{5,6},{6,7},{7,8},{8,9},{9,10},{10,1... | collective-permute-start | bytes 1544 | tf_op jit(solution)/shard_map/while/body/eval_jaxpr/ppermute | solution.py:24
  178.9 5.6 %collective-permute-start = (f32[1,128]{1,0:T(1,128)S(1)}, f32[1,128]{1,0:T(1,128)S(1)}, u32[]{:S(2)}, u32[]{:S(2)}) collective-permute-start(f32[1,128]{1,0:T(1,128)S(1)} %broadcast_select_fusion.2), channel_id=1, source_target_pairs={{0,1},{1,2},{2,3},{3,4},{4,5},{5,6},{6,7},{7,8},{8,9},{9,10},{10,1... | collective-permute-start | bytes 1544 | tf_op jit(solution)/shard_map/while/body/eval_jaxpr/ppermute | solution.py:24
  186.7 5.6 %collective-permute-start = (f32[1,128]{1,0:T(1,128)S(1)}, f32[1,128]{1,0:T(1,128)S(1)}, u32[]{:S(2)}, u32[]{:S(2)}) collective-permute-start(f32[1,128]{1,0:T(1,128)S(1)} %broadcast_select_fusion.2), channel_id=1, source_target_pairs={{0,1},{1,2},{2,3},{3,4},{4,5},{5,6},{6,7},{7,8},{8,9},{9,10},{10,1... | collective-permute-start | bytes 1544 | tf_op jit(solution)/shard_map/while/body/eval_jaxpr/ppermute | solution.py:24
  194.5 5.6 %collective-permute-start = (f32[1,128]{1,0:T(1,128)S(1)}, f32[1,128]{1,0:T(1,128)S(1)}, u32[]{:S(2)}, u32[]{:S(2)}) collective-permute-start(f32[1,128]{1,0:T(1,128)S(1)} %broadcast_select_fusion.2), channel_id=1, source_target_pairs={{0,1},{1,2},{2,3},{3,4},{4,5},{5,6},{6,7},{7,8},{8,9},{9,10},{10,1... | collective-permute-start | bytes 1544 | tf_op jit(solution)/shard_map/while/body/eval_jaxpr/ppermute | solution.py:24
  202.2 5.6 %collective-permute-start = (f32[1,128]{1,0:T(1,128)S(1)}, f32[1,128]{1,0:T(1,128)S(1)}, u32[]{:S(2)}, u32[]{:S(2)}) collective-permute-start(f32[1,128]{1,0:T(1,128)S(1)} %broadcast_select_fusion.2), channel_id=1, source_target_pairs={{0,1},{1,2},{2,3},{3,4},{4,5},{5,6},{6,7},{7,8},{8,9},{9,10},{10,1... | collective-permute-start | bytes 1544 | tf_op jit(solution)/shard_map/while/body/eval_jaxpr/ppermute | solution.py:24
  210.0 5.6 %collective-permute-start = (f32[1,128]{1,0:T(1,128)S(1)}, f32[1,128]{1,0:T(1,128)S(1)}, u32[]{:S(2)}, u32[]{:S(2)}) collective-permute-start(f32[1,128]{1,0:T(1,128)S(1)} %broadcast_select_fusion.2), channel_id=1, source_target_pairs={{0,1},{1,2},{2,3},{3,4},{4,5},{5,6},{6,7},{7,8},{8,9},{9,10},{10,1... | collective-permute-start | bytes 1544 | tf_op jit(solution)/shard_map/while/body/eval_jaxpr/ppermute | solution.py:24
  217.8 5.6 %collective-permute-start = (f32[1,128]{1,0:T(1,128)S(1)}, f32[1,128]{1,0:T(1,128)S(1)}, u32[]{:S(2)}, u32[]{:S(2)}) collective-permute-start(f32[1,128]{1,0:T(1,128)S(1)} %broadcast_select_fusion.2), channel_id=1, source_target_pairs={{0,1},{1,2},{2,3},{3,4},{4,5},{5,6},{6,7},{7,8},{8,9},{9,10},{10,1... | collective-permute-start | bytes 1544 | tf_op jit(solution)/shard_map/while/body/eval_jaxpr/ppermute | solution.py:24
  225.5 5.6 %collective-permute-start = (f32[1,128]{1,0:T(1,128)S(1)}, f32[1,128]{1,0:T(1,128)S(1)}, u32[]{:S(2)}, u32[]{:S(2)}) collective-permute-start(f32[1,128]{1,0:T(1,128)S(1)} %broadcast_select_fusion.2), channel_id=1, source_target_pairs={{0,1},{1,2},{2,3},{3,4},{4,5},{5,6},{6,7},{7,8},{8,9},{9,10},{10,1... | collective-permute-start | bytes 1544 | tf_op jit(solution)/shard_map/while/body/eval_jaxpr/ppermute | solution.py:24
  233.3 5.6 %collective-permute-start = (f32[1,128]{1,0:T(1,128)S(1)}, f32[1,128]{1,0:T(1,128)S(1)}, u32[]{:S(2)}, u32[]{:S(2)}) collective-permute-start(f32[1,128]{1,0:T(1,128)S(1)} %broadcast_select_fusion.2), channel_id=1, source_target_pairs={{0,1},{1,2},{2,3},{3,4},{4,5},{5,6},{6,7},{7,8},{8,9},{9,10},{10,1... | collective-permute-start | bytes 1544 | tf_op jit(solution)/shard_map/while/body/eval_jaxpr/ppermute | solution.py:24
  241.1 5.6 %collective-permute-start = (f32[1,128]{1,0:T(1,128)S(1)}, f32[1,128]{1,0:T(1,128)S(1)}, u32[]{:S(2)}, u32[]{:S(2)}) collective-permute-start(f32[1,128]{1,0:T(1,128)S(1)} %broadcast_select_fusion.2), channel_id=1, source_target_pairs={{0,1},{1,2},{2,3},{3,4},{4,5},{5,6},{6,7},{7,8},{8,9},{9,10},{10,1... | collective-permute-start | bytes 1544 | tf_op jit(solution)/shard_map/while/body/eval_jaxpr/ppermute | solution.py:24
  248.9 5.6 %collective-permute-start = (f32[1,128]{1,0:T(1,128)S(1)}, f32[1,128]{1,0:T(1,128)S(1)}, u32[]{:S(2)}, u32[]{:S(2)}) collective-permute-start(f32[1,128]{1,0:T(1,128)S(1)} %broadcast_select_fusion.2), channel_id=1, source_target_pairs={{0,1},{1,2},{2,3},{3,4},{4,5},{5,6},{6,7},{7,8},{8,9},{9,10},{10,1... | collective-permute-start | bytes 1544 | tf_op jit(solution)/shard_map/while/body/eval_jaxpr/ppermute | solution.py:24
  256.6 5.6 %collective-permute-start = (f32[1,128]{1,0:T(1,128)S(1)}, f32[1,128]{1,0:T(1,128)S(1)}, u32[]{:S(2)}, u32[]{:S(2)}) collective-permute-start(f32[1,128]{1,0:T(1,128)S(1)} %broadcast_select_fusion.2), channel_id=1, source_target_pairs={{0,1},{1,2},{2,3},{3,4},{4,5},{5,6},{6,7},{7,8},{8,9},{9,10},{10,1... | collective-permute-start | bytes 1544 | tf_op jit(solution)/shard_map/while/body/eval_jaxpr/ppermute | solution.py:24
  264.4 5.6 %collective-permute-start = (f32[1,128]{1,0:T(1,128)S(1)}, f32[1,128]{1,0:T(1,128)S(1)}, u32[]{:S(2)}, u32[]{:S(2)}) collective-permute-start(f32[1,128]{1,0:T(1,128)S(1)} %broadcast_select_fusion.2), channel_id=1, source_target_pairs={{0,1},{1,2},{2,3},{3,4},{4,5},{5,6},{6,7},{7,8},{8,9},{9,10},{10,1... | collective-permute-start | bytes 1544 | tf_op jit(solution)/shard_map/while/body/eval_jaxpr/ppermute | solution.py:24
  272.4 5.6 %collective-permute-start.28 = (f32[1,256]{1,0:T(1,128)S(1)}, f32[1,256]{1,0:T(1,128)S(1)}, u32[]{:S(2)}, u32[]{:S(2)}) collective-permute-start(f32[1,256]{1,0:T(1,128)S(1)} %get-tuple-element.261), channel_id=1, source_target_pairs={{0,1},{1,2},{2,3},{3,4},{4,5},{5,6},{6,7},{7,8},{8,9},{9,10},{10,1... | collective-permute-start | bytes 3080 | tf_op jit(solution)/shard_map/ppermute | solution.py:24
  280.2 5.6 %collective-permute-start.30 = (f32[1,256]{1,0:T(1,128)S(1)}, f32[1,256]{1,0:T(1,128)S(1)}, u32[]{:S(2)}, u32[]{:S(2)}) collective-permute-start(f32[1,256]{1,0:T(1,128)S(1)} %get-tuple-element.257), channel_id=1, source_target_pairs={{0,1},{1,2},{2,3},{3,4},{4,5},{5,6},{6,7},{7,8},{8,9},{9,10},{10,1... | collective-permute-start | bytes 3080 | tf_op jit(solution)/shard_map/ppermute | solution.py:24
  288.4 5.6 %collective-permute-start.32 = (f32[1,512]{1,0:T(1,128)S(1)}, f32[1,512]{1,0:T(1,128)S(1)}, u32[]{:S(2)}, u32[]{:S(2)}) collective-permute-start(f32[1,512]{1,0:T(1,128)S(1)} %get-tuple-element.245), channel_id=1, source_target_pairs={{0,1},{1,2},{2,3},{3,4},{4,5},{5,6},{6,7},{7,8},{8,9},{9,10},{10,1... | collective-permute-start | bytes 6152 | tf_op jit(solution)/shard_map/ppermute | solution.py:24
  296.2 5.8 %collective-permute-start.34 = (f32[1,512]{1,0:T(1,128)S(1)}, f32[1,512]{1,0:T(1,128)S(1)}, u32[]{:S(2)}, u32[]{:S(2)}) collective-permute-start(f32[1,512]{1,0:T(1,128)S(1)} %get-tuple-element.241), channel_id=1, source_target_pairs={{0,1},{1,2},{2,3},{3,4},{4,5},{5,6},{6,7},{7,8},{8,9},{9,10},{10,1... | collective-permute-start | bytes 6152 | tf_op jit(solution)/shard_map/ppermute | solution.py:24
  305.6 5.6 %collective-permute-start.36 = (f32[1,1024]{1,0:T(1,128)S(1)}, f32[1,1024]{1,0:T(1,128)S(1)}, u32[]{:S(2)}, u32[]{:S(2)}) collective-permute-start(f32[1,1024]{1,0:T(1,128)S(1)} %get-tuple-element.229), channel_id=1, source_target_pairs={{0,1},{1,2},{2,3},{3,4},{4,5},{5,6},{6,7},{7,8},{8,9},{9,10},{10,1... | collective-permute-start | bytes 12296 | tf_op jit(solution)/shard_map/ppermute | solution.py:24
  313.4 5.6 %collective-permute-start.38 = (f32[1,1024]{1,0:T(1,128)S(1)}, f32[1,1024]{1,0:T(1,128)S(1)}, u32[]{:S(2)}, u32[]{:S(2)}) collective-permute-start(f32[1,1024]{1,0:T(1,128)S(1)} %get-tuple-element.225), channel_id=1, source_target_pairs={{0,1},{1,2},{2,3},{3,4},{4,5},{5,6},{6,7},{7,8},{8,9},{9,10},{10,1... | collective-permute-start | bytes 12296 | tf_op jit(solution)/shard_map/ppermute | solution.py:24
  323.8 8.7 %reshape.117 = f32[16,2048]{1,0:T(8,128)S(1)} reshape(f32[8,2,1024,2]{3,2,1,0:T(8,128)} %broadcast_in_dim.65) | data formatting | bytes 262144 | tf_op jit(solution)/shard_map/reshape | solution.py:84
  333.9 5.6 %collective-permute-start.40 = (f32[1,2048]{1,0:T(1,128)S(1)}, f32[1,2048]{1,0:T(1,128)S(1)}, u32[]{:S(2)}, u32[]{:S(2)}) collective-permute-start(f32[1,2048]{1,0:T(1,128)S(1)} %get-tuple-element.211), channel_id=1, source_target_pairs={{0,1},{1,2},{2,3},{3,4},{4,5},{5,6},{6,7},{7,8},{8,9},{9,10},{10,1... | collective-permute-start | bytes 24584 | tf_op jit(solution)/shard_map/ppermute | solution.py:24
  341.9 5.7 %collective-permute-start.42 = (f32[1,2048]{1,0:T(1,128)S(1)}, f32[1,2048]{1,0:T(1,128)S(1)}, u32[]{:S(2)}, u32[]{:S(2)}) collective-permute-start(f32[1,2048]{1,0:T(1,128)S(1)} %get-tuple-element.207), channel_id=1, source_target_pairs={{0,1},{1,2},{2,3},{3,4},{4,5},{5,6},{6,7},{7,8},{8,9},{9,10},{10,1... | collective-permute-start | bytes 24584 | tf_op jit(solution)/shard_map/ppermute | solution.py:24
  349.2 75.7 %while.14 = (s32[]{:T(128)}, f32[40,2048]{1,0:T(8,128)S(1)}, s32[40,2]{0,1:T(2,128)S(1)}, f32[40,128]{1,0:T(8,128)S(1)}, s32[]{:T(128)}, /*index=5*/s32[]{:T(128)}) while((s32[]{:T(128)}, f32[40,2048]{1,0:T(8,128)S(1)}, s32[40,2]{0,1:T(2,128)S(1)}, f32[40,128]{1,0:T(8,128)S(1)}, s32[]{:T(128)}, /*index=5*/s32[]{:T(128)}) %tuple.91), condition=%wide.while_cond, body=%wide.while_body.sunk | while | flops 2 | bytes 2169 | solution.py:128
  425.0 28.8 %all_gather.11 = f32[640,128]{1,0:T(8,128)S(1)} all-gather(f32[40,128]{1,0:T(8,128)S(1)} %mul.503), channel_id=1, replica_groups=mesh['real'=2,'tx'=16] {'tx'}, dimensions={0}, use_global_device_ids=true | all-gather | bytes 348160 | tf_op jit(solution)/shard_map/all_gather | solution.py:134
  (489 shorter events, 241.9 us)
Async XLA Ops:
  0.7 60.2 %collective-permute-start.4 = (f32[1,2048]{1,0:T(1,128)S(1)}, f32[1,2048]{1,0:T(1,128)S(1)}, u32[]{:S(2)}, u32[]{:S(2)}) collective-permute-start(f32[1,2048]{1,0:T(1,128)S(1)} %broadcast.163), channel_id=1, source_target_pairs={{0,1},{1,2},{2,3},{3,4},{4,5},{5,6},{6,7},{7,8},{8,9},{9,10},{10,1... | collective-permute-start | bytes 24584 | tf_op jit(solution)/shard_map/ppermute | solution.py:24
  3.1 57.7 %collective-permute-start.2 = (f32[1,2048]{1,0:T(1,128)S(1)}, f32[1,2048]{1,0:T(1,128)S(1)}, u32[]{:S(2)}, u32[]{:S(2)}) collective-permute-start(f32[1,2048]{1,0:T(1,128)S(1)} %broadcast.163), channel_id=1, source_target_pairs={{1,0},{2,1},{3,2},{4,3},{5,4},{6,5},{7,6},{8,7},{9,8},{10,9},{11,1... | collective-permute-start | bytes 24584 | tf_op jit(solution)/shard_map/ppermute | solution.py:26
  4.5 128.1 %collective-permute-start.22 = (f32[1,256]{1,0:T(1,128)S(1)}, f32[1,256]{1,0:T(1,128)S(1)}, u32[]{:S(2)}, u32[]{:S(2)}) collective-permute-start(f32[1,256]{1,0:T(1,128)S(1)} %broadcast.172), channel_id=1, source_target_pairs={{0,1},{1,2},{2,3},{3,4},{4,5},{5,6},{6,7},{7,8},{8,9},{9,10},{10,1... | collective-permute-start | bytes 3080 | tf_op jit(solution)/shard_map/ppermute | solution.py:24
  10.5 50.4 %collective-permute-start.3 = (f32[1,2048]{1,0:T(1,128)S(1)}, f32[1,2048]{1,0:T(1,128)S(1)}, u32[]{:S(2)}, u32[]{:S(2)}) collective-permute-start(f32[1,2048]{1,0:T(1,128)S(1)} %slice.446), channel_id=1, source_target_pairs={{0,1},{1,2},{2,3},{3,4},{4,5},{5,6},{6,7},{7,8},{8,9},{9,10},{10,1... | collective-permute-start | bytes 24584 | tf_op jit(solution)/shard_map/ppermute | solution.py:36
  59.6 73.1 %collective-permute-start.21 = (f32[1,256]{1,0:T(1,128)S(1)}, f32[1,256]{1,0:T(1,128)S(1)}, u32[]{:S(2)}, u32[]{:S(2)}) collective-permute-start(f32[1,256]{1,0:T(1,128)S(1)} %broadcast.172), channel_id=1, source_target_pairs={{1,0},{2,1},{3,2},{4,3},{5,4},{6,5},{7,6},{8,7},{9,8},{10,9},{11,1... | collective-permute-start | bytes 3080 | tf_op jit(solution)/shard_map/ppermute | solution.py:26
  61.1 8.0 %collective-permute-start.5 = (f32[1,2048]{1,0:T(1,128)S(1)}, f32[1,2048]{1,0:T(1,128)S(1)}, u32[]{:S(2)}, u32[]{:S(2)}) collective-permute-start(f32[1,2048]{1,0:T(1,128)S(1)} %get-tuple-element.220), channel_id=1, source_target_pairs={{1,0},{2,1},{3,2},{4,3},{5,4},{6,5},{7,6},{8,7},{9,8},{10,9},{11,1... | collective-permute-start | bytes 24584 | tf_op jit(solution)/shard_map/ppermute | solution.py:26
  69.3 9.3 %collective-permute-start.7 = (f32[1,2048]{1,0:T(1,128)S(1)}, f32[1,2048]{1,0:T(1,128)S(1)}, u32[]{:S(2)}, u32[]{:S(2)}) collective-permute-start(f32[1,2048]{1,0:T(1,128)S(1)} %get-tuple-element.216), channel_id=1, source_target_pairs={{1,0},{2,1},{3,2},{4,3},{5,4},{6,5},{7,6},{8,7},{9,8},{10,9},{11,1... | collective-permute-start | bytes 24584 | tf_op jit(solution)/shard_map/ppermute | solution.py:26
  70.6 9.4 %collective-permute-start.8 = (f32[1,2048]{1,0:T(1,128)S(1)}, f32[1,2048]{1,0:T(1,128)S(1)}, u32[]{:S(2)}, u32[]{:S(2)}) collective-permute-start(f32[1,2048]{1,0:T(1,128)S(1)} %get-tuple-element.217), channel_id=1, source_target_pairs={{0,1},{1,2},{2,3},{3,4},{4,5},{5,6},{6,7},{7,8},{8,9},{9,10},{10,1... | collective-permute-start | bytes 24584 | tf_op jit(solution)/shard_map/ppermute | solution.py:24
  75.0 20.2 %collective-permute-start.10 = (f32[1,1024]{1,0:T(1,128)S(1)}, f32[1,1024]{1,0:T(1,128)S(1)}, u32[]{:S(2)}, u32[]{:S(2)}) collective-permute-start(f32[1,1024]{1,0:T(1,128)S(1)} %broadcast.166), channel_id=1, source_target_pairs={{0,1},{1,2},{2,3},{3,4},{4,5},{5,6},{6,7},{7,8},{8,9},{9,10},{10,1... | collective-permute-start | bytes 12296 | tf_op jit(solution)/shard_map/ppermute | solution.py:24
  78.7 16.5 %collective-permute-start.9 = (f32[1,1024]{1,0:T(1,128)S(1)}, f32[1,1024]{1,0:T(1,128)S(1)}, u32[]{:S(2)}, u32[]{:S(2)}) collective-permute-start(f32[1,1024]{1,0:T(1,128)S(1)} %broadcast.166), channel_id=1, source_target_pairs={{1,0},{2,1},{3,2},{4,3},{5,4},{6,5},{7,6},{8,7},{9,8},{10,9},{11,1... | collective-permute-start | bytes 12296 | tf_op jit(solution)/shard_map/ppermute | solution.py:26
  102.9 10.7 %collective-permute-start.13 = (f32[1,1024]{1,0:T(1,128)S(1)}, f32[1,1024]{1,0:T(1,128)S(1)}, u32[]{:S(2)}, u32[]{:S(2)}) collective-permute-start(f32[1,1024]{1,0:T(1,128)S(1)} %get-tuple-element.232), channel_id=1, source_target_pairs={{1,0},{2,1},{3,2},{4,3},{5,4},{6,5},{7,6},{8,7},{9,8},{10,9},{11,1... | collective-permute-start | bytes 12296 | tf_op jit(solution)/shard_map/ppermute | solution.py:26
  104.2 10.7 %collective-permute-start.14 = (f32[1,1024]{1,0:T(1,128)S(1)}, f32[1,1024]{1,0:T(1,128)S(1)}, u32[]{:S(2)}, u32[]{:S(2)}) collective-permute-start(f32[1,1024]{1,0:T(1,128)S(1)} %get-tuple-element.233), channel_id=1, source_target_pairs={{0,1},{1,2},{2,3},{3,4},{4,5},{5,6},{6,7},{7,8},{8,9},{9,10},{10,1... | collective-permute-start | bytes 12296 | tf_op jit(solution)/shard_map/ppermute | solution.py:24
  109.4 8.1 %collective-permute-start.16 = (f32[1,512]{1,0:T(1,128)S(1)}, f32[1,512]{1,0:T(1,128)S(1)}, u32[]{:S(2)}, u32[]{:S(2)}) collective-permute-start(f32[1,512]{1,0:T(1,128)S(1)} %broadcast.169), channel_id=1, source_target_pairs={{0,1},{1,2},{2,3},{3,4},{4,5},{5,6},{6,7},{7,8},{8,9},{9,10},{10,1... | collective-permute-start | bytes 6152 | tf_op jit(solution)/shard_map/ppermute | solution.py:24
  117.5 7.2 %collective-permute-start.17 = (f32[1,512]{1,0:T(1,128)S(1)}, f32[1,512]{1,0:T(1,128)S(1)}, u32[]{:S(2)}, u32[]{:S(2)}) collective-permute-start(f32[1,512]{1,0:T(1,128)S(1)} %get-tuple-element.252), channel_id=1, source_target_pairs={{1,0},{2,1},{3,2},{4,3},{5,4},{6,5},{7,6},{8,7},{9,8},{10,9},{11,1... | collective-permute-start | bytes 6152 | tf_op jit(solution)/shard_map/ppermute | solution.py:26
  154.2 7.0 %collective-permute-start.1 = (f32[1,128]{1,0:T(1,128)S(1)}, f32[1,128]{1,0:T(1,128)S(1)}, u32[]{:S(2)}, u32[]{:S(2)}) collective-permute-start(f32[1,128]{1,0:T(1,128)S(1)} %broadcast_select_fusion.2), channel_id=1, source_target_pairs={{1,0},{2,1},{3,2},{4,3},{5,4},{6,5},{7,6},{8,7},{9,8},{10,9},{11,1... | collective-permute-start | bytes 1544 | tf_op jit(solution)/shard_map/while/body/eval_jaxpr/ppermute | solution.py:26
  162.0 7.0 %collective-permute-start.1 = (f32[1,128]{1,0:T(1,128)S(1)}, f32[1,128]{1,0:T(1,128)S(1)}, u32[]{:S(2)}, u32[]{:S(2)}) collective-permute-start(f32[1,128]{1,0:T(1,128)S(1)} %broadcast_select_fusion.2), channel_id=1, source_target_pairs={{1,0},{2,1},{3,2},{4,3},{5,4},{6,5},{7,6},{8,7},{9,8},{10,9},{11,1... | collective-permute-start | bytes 1544 | tf_op jit(solution)/shard_map/while/body/eval_jaxpr/ppermute | solution.py:26
  169.8 7.0 %collective-permute-start.1 = (f32[1,128]{1,0:T(1,128)S(1)}, f32[1,128]{1,0:T(1,128)S(1)}, u32[]{:S(2)}, u32[]{:S(2)}) collective-permute-start(f32[1,128]{1,0:T(1,128)S(1)} %broadcast_select_fusion.2), channel_id=1, source_target_pairs={{1,0},{2,1},{3,2},{4,3},{5,4},{6,5},{7,6},{8,7},{9,8},{10,9},{11,1... | collective-permute-start | bytes 1544 | tf_op jit(solution)/shard_map/while/body/eval_jaxpr/ppermute | solution.py:26
  177.6 7.0 %collective-permute-start.1 = (f32[1,128]{1,0:T(1,128)S(1)}, f32[1,128]{1,0:T(1,128)S(1)}, u32[]{:S(2)}, u32[]{:S(2)}) collective-permute-start(f32[1,128]{1,0:T(1,128)S(1)} %broadcast_select_fusion.2), channel_id=1, source_target_pairs={{1,0},{2,1},{3,2},{4,3},{5,4},{6,5},{7,6},{8,7},{9,8},{10,9},{11,1... | collective-permute-start | bytes 1544 | tf_op jit(solution)/shard_map/while/body/eval_jaxpr/ppermute | solution.py:26
  185.4 7.0 %collective-permute-start.1 = (f32[1,128]{1,0:T(1,128)S(1)}, f32[1,128]{1,0:T(1,128)S(1)}, u32[]{:S(2)}, u32[]{:S(2)}) collective-permute-start(f32[1,128]{1,0:T(1,128)S(1)} %broadcast_select_fusion.2), channel_id=1, source_target_pairs={{1,0},{2,1},{3,2},{4,3},{5,4},{6,5},{7,6},{8,7},{9,8},{10,9},{11,1... | collective-permute-start | bytes 1544 | tf_op jit(solution)/shard_map/while/body/eval_jaxpr/ppermute | solution.py:26
  193.2 7.0 %collective-permute-start.1 = (f32[1,128]{1,0:T(1,128)S(1)}, f32[1,128]{1,0:T(1,128)S(1)}, u32[]{:S(2)}, u32[]{:S(2)}) collective-permute-start(f32[1,128]{1,0:T(1,128)S(1)} %broadcast_select_fusion.2), channel_id=1, source_target_pairs={{1,0},{2,1},{3,2},{4,3},{5,4},{6,5},{7,6},{8,7},{9,8},{10,9},{11,1... | collective-permute-start | bytes 1544 | tf_op jit(solution)/shard_map/while/body/eval_jaxpr/ppermute | solution.py:26
  208.7 7.0 %collective-permute-start.1 = (f32[1,128]{1,0:T(1,128)S(1)}, f32[1,128]{1,0:T(1,128)S(1)}, u32[]{:S(2)}, u32[]{:S(2)}) collective-permute-start(f32[1,128]{1,0:T(1,128)S(1)} %broadcast_select_fusion.2), channel_id=1, source_target_pairs={{1,0},{2,1},{3,2},{4,3},{5,4},{6,5},{7,6},{8,7},{9,8},{10,9},{11,1... | collective-permute-start | bytes 1544 | tf_op jit(solution)/shard_map/while/body/eval_jaxpr/ppermute | solution.py:26
  216.5 7.0 %collective-permute-start.1 = (f32[1,128]{1,0:T(1,128)S(1)}, f32[1,128]{1,0:T(1,128)S(1)}, u32[]{:S(2)}, u32[]{:S(2)}) collective-permute-start(f32[1,128]{1,0:T(1,128)S(1)} %broadcast_select_fusion.2), channel_id=1, source_target_pairs={{1,0},{2,1},{3,2},{4,3},{5,4},{6,5},{7,6},{8,7},{9,8},{10,9},{11,1... | collective-permute-start | bytes 1544 | tf_op jit(solution)/shard_map/while/body/eval_jaxpr/ppermute | solution.py:26
  224.3 7.0 %collective-permute-start.1 = (f32[1,128]{1,0:T(1,128)S(1)}, f32[1,128]{1,0:T(1,128)S(1)}, u32[]{:S(2)}, u32[]{:S(2)}) collective-permute-start(f32[1,128]{1,0:T(1,128)S(1)} %broadcast_select_fusion.2), channel_id=1, source_target_pairs={{1,0},{2,1},{3,2},{4,3},{5,4},{6,5},{7,6},{8,7},{9,8},{10,9},{11,1... | collective-permute-start | bytes 1544 | tf_op jit(solution)/shard_map/while/body/eval_jaxpr/ppermute | solution.py:26
  232.0 7.0 %collective-permute-start.1 = (f32[1,128]{1,0:T(1,128)S(1)}, f32[1,128]{1,0:T(1,128)S(1)}, u32[]{:S(2)}, u32[]{:S(2)}) collective-permute-start(f32[1,128]{1,0:T(1,128)S(1)} %broadcast_select_fusion.2), channel_id=1, source_target_pairs={{1,0},{2,1},{3,2},{4,3},{5,4},{6,5},{7,6},{8,7},{9,8},{10,9},{11,1... | collective-permute-start | bytes 1544 | tf_op jit(solution)/shard_map/while/body/eval_jaxpr/ppermute | solution.py:26
  271.1 7.0 %collective-permute-start.27 = (f32[1,256]{1,0:T(1,128)S(1)}, f32[1,256]{1,0:T(1,128)S(1)}, u32[]{:S(2)}, u32[]{:S(2)}) collective-permute-start(f32[1,256]{1,0:T(1,128)S(1)} %get-tuple-element.260), channel_id=1, source_target_pairs={{1,0},{2,1},{3,2},{4,3},{5,4},{6,5},{7,6},{8,7},{9,8},{10,9},{11,1... | collective-permute-start | bytes 3080 | tf_op jit(solution)/shard_map/ppermute | solution.py:26
  278.9 7.0 %collective-permute-start.29 = (f32[1,256]{1,0:T(1,128)S(1)}, f32[1,256]{1,0:T(1,128)S(1)}, u32[]{:S(2)}, u32[]{:S(2)}) collective-permute-start(f32[1,256]{1,0:T(1,128)S(1)} %get-tuple-element.256), channel_id=1, source_target_pairs={{1,0},{2,1},{3,2},{4,3},{5,4},{6,5},{7,6},{8,7},{9,8},{10,9},{11,1... | collective-permute-start | bytes 3080 | tf_op jit(solution)/shard_map/ppermute | solution.py:26
  287.1 7.0 %collective-permute-start.31 = (f32[1,512]{1,0:T(1,128)S(1)}, f32[1,512]{1,0:T(1,128)S(1)}, u32[]{:S(2)}, u32[]{:S(2)}) collective-permute-start(f32[1,512]{1,0:T(1,128)S(1)} %get-tuple-element.244), channel_id=1, source_target_pairs={{1,0},{2,1},{3,2},{4,3},{5,4},{6,5},{7,6},{8,7},{9,8},{10,9},{11,1... | collective-permute-start | bytes 6152 | tf_op jit(solution)/shard_map/ppermute | solution.py:26
  294.9 7.2 %collective-permute-start.33 = (f32[1,512]{1,0:T(1,128)S(1)}, f32[1,512]{1,0:T(1,128)S(1)}, u32[]{:S(2)}, u32[]{:S(2)}) collective-permute-start(f32[1,512]{1,0:T(1,128)S(1)} %get-tuple-element.240), channel_id=1, source_target_pairs={{1,0},{2,1},{3,2},{4,3},{5,4},{6,5},{7,6},{8,7},{9,8},{10,9},{11,1... | collective-permute-start | bytes 6152 | tf_op jit(solution)/shard_map/ppermute | solution.py:26
  304.3 7.0 %collective-permute-start.35 = (f32[1,1024]{1,0:T(1,128)S(1)}, f32[1,1024]{1,0:T(1,128)S(1)}, u32[]{:S(2)}, u32[]{:S(2)}) collective-permute-start(f32[1,1024]{1,0:T(1,128)S(1)} %get-tuple-element.228), channel_id=1, source_target_pairs={{1,0},{2,1},{3,2},{4,3},{5,4},{6,5},{7,6},{8,7},{9,8},{10,9},{11,1... | collective-permute-start | bytes 12296 | tf_op jit(solution)/shard_map/ppermute | solution.py:26
  312.1 7.0 %collective-permute-start.37 = (f32[1,1024]{1,0:T(1,128)S(1)}, f32[1,1024]{1,0:T(1,128)S(1)}, u32[]{:S(2)}, u32[]{:S(2)}) collective-permute-start(f32[1,1024]{1,0:T(1,128)S(1)} %get-tuple-element.224), channel_id=1, source_target_pairs={{1,0},{2,1},{3,2},{4,3},{5,4},{6,5},{7,6},{8,7},{9,8},{10,9},{11,1... | collective-permute-start | bytes 12296 | tf_op jit(solution)/shard_map/ppermute | solution.py:26
  332.6 7.0 %collective-permute-start.39 = (f32[1,2048]{1,0:T(1,128)S(1)}, f32[1,2048]{1,0:T(1,128)S(1)}, u32[]{:S(2)}, u32[]{:S(2)}) collective-permute-start(f32[1,2048]{1,0:T(1,128)S(1)} %get-tuple-element.210), channel_id=1, source_target_pairs={{1,0},{2,1},{3,2},{4,3},{5,4},{6,5},{7,6},{8,7},{9,8},{10,9},{11,1... | collective-permute-start | bytes 24584 | tf_op jit(solution)/shard_map/ppermute | solution.py:26
  340.6 7.1 %collective-permute-start.41 = (f32[1,2048]{1,0:T(1,128)S(1)}, f32[1,2048]{1,0:T(1,128)S(1)}, u32[]{:S(2)}, u32[]{:S(2)}) collective-permute-start(f32[1,2048]{1,0:T(1,128)S(1)} %get-tuple-element.206), channel_id=1, source_target_pairs={{1,0},{2,1},{3,2},{4,3},{5,4},{6,5},{7,6},{8,7},{9,8},{10,9},{11,1... | collective-permute-start | bytes 24584 | tf_op jit(solution)/shard_map/ppermute | solution.py:26
  (47 other events, 530.6 us)
where the time goes:
time: 458 us; the launch traced here: 455 us
  starting transfers between devices  236 us (52%)
  local copies, waits for them, and re-layouts  134 us (29%)
  blocking collectives  40.6 us (9%)
  waiting for transfers between devices  20.9 us (5%)
  other arithmetic  19.5 us (4%)
    ppermute x36, starting transfers between devices, padded_2(): lax.ppermute(tail, axis, [(i, (i + 1) % count) for i in range(ends)])  186 us
    gather x160, local copies, waits for them, and re-layouts  75.6 us
    ppermute x36, starting transfers between devices, padded_2(): lax.ppermute(head, axis, [((i + 1) % count, i) for i in range(ends)])  46.4 us
    all_gather x1, blocking collectives, shards(): piece_terms = lax.all_gather(terms, 'tx', axis=0, tiled=True)  28.8 us
    ppermute x36, waiting for transfers between devices, padded_2(): lax.ppermute(tail, axis, [(i, (i + 1) % count) for i in range(ends)])  20.8 us
    reshape x3, local copies, waits for them, and re-layouts, coarsen(): coarse_store = storage.reshape(rows // 2, 2, cols // 2, 2).sum(axis=(1, 3))  13.1 us
    reshape x3, local copies, waits for them, and re-layouts, restrict(): return field.reshape(rows // 2, 2, cols // 2, 2).sum(axis=(1, 3))  13.1 us
    unnamed x1, blocking collectives  11.8 us
  transfers between devices with their start and end apart: 73, of which 29 were waited for; matrix products, arithmetic and copies ran while one was open for 13% of the time, Pallas kernels for 0%

commit v1 on v0

v1 whole, which is shorter than its diff:
```python
import functools

import jax
import jax.numpy as jnp
from jax import lax
from jax.experimental import pallas as pl
from jax.experimental.pallas import tpu as pltpu
from jax.sharding import PartitionSpec as P

BLK_DEV = 8
SCREEN = 128
CSW = 16
OMEGA = 0.8
F32 = jnp.float32


def iota(shape, dim):
    return lax.broadcasted_iota(jnp.int32, shape, dim)


def dot(a, b):
    return lax.dot_general(
        a, b, (((1,), (0,)), ((), ())), precision=lax.Precision.HIGHEST, preferred_element_type=F32
    )


def roll(x, shift, axis):
    shift = shift % x.shape[axis]
    return x if shift == 0 else pltpu.roll(x, shift, axis)


def pair_cols(x, odd_only=False):
    rows, cols = x.shape
    i, j = iota((256, 128), 0), iota((256, 128), 1)
    pick = (i == 2 * j + 1) if odd_only else (i // 2 == j)
    chunks = cols // 256
    stacked = jnp.concatenate([x[:, 256 * c : 256 * c + 256] for c in range(chunks)], axis=0)
    y = dot(stacked, pick.astype(F32))
    return jnp.concatenate([y[rows * c : rows * (c + 1)] for c in range(chunks)], axis=1)


def twice_cols(x):
    rows, cols = x.shape
    i, j = iota((128, 256), 0), iota((128, 256), 1)
    chunks = cols // 128
    stacked = jnp.concatenate([x[:, 128 * c : 128 * c + 128] for c in range(chunks)], axis=0)
    y = dot(stacked, (j // 2 == i).astype(F32))
    return jnp.concatenate([y[rows * c : rows * (c + 1)] for c in range(chunks)], axis=1)


def rows_by(pick, x):
    return dot(pick.astype(F32), x)


def coefficients(s, ax, ay, live, whole=False):
    rows, cols = s.shape
    row, col = iota((rows, cols), 0), iota((rows, cols), 1)
    bx = roll(ax, 1, 0)
    if whole:
        bx = jnp.where(row == 0, 0.0, bx)
    by = jnp.where(col == 0, 0.0, roll(ay, 1, 1))
    diag = s + ax + bx + ay + by
    w = OMEGA / diag
    if live is not None:
        w = jnp.where(live, w, 0.0)
    cu = w * ax
    if whole:
        cu = jnp.where(row == rows - 1, 0.0, cu)
    cr = jnp.where(col == cols - 1, 0.0, w * ay)
    return (w, cu, w * bx, cr, w * by, diag * (1.0 / OMEGA))


def sweep(u, wb, c):
    return (
        (1.0 - OMEGA) * u
        + wb
        + c[1] * roll(u, -1, 0)
        + c[2] * roll(u, 1, 0)
        + c[3] * roll(u, -1, 1)
        + c[4] * roll(u, 1, 1)
    )


def coefficients_split(s, ax, ay):
    rows, cols = s[0].shape
    row, col = iota((rows, cols), 0), iota((rows, cols), 1)
    bx = (jnp.where(row == 0, 0.0, roll(ax[1], 1, 0)), ax[0])
    out = []
    for h in range(2):
        by = jnp.where(col == 0, 0.0, roll(ay[h], 1, 1))
        diag = s[h] + ax[h] + bx[h] + ay[h] + by
        w = OMEGA / diag
        cu = w * ax[h] if h == 0 else jnp.where(row == rows - 1, 0.0, w * ax[h])
        cr = jnp.where(col == cols - 1, 0.0, w * ay[h])
        out.append((w, cu, w * bx[h], cr, w * by, diag * (1.0 / OMEGA)))
    return out


def sweep_split(u, wb, c):
    upper = (u[1], roll(u[0], -1, 0))
    lower = (roll(u[1], 1, 0), u[0])
    return tuple(
        (1.0 - OMEGA) * u[h]
        + wb[h]
        + c[h][1] * upper[h]
        + c[h][2] * lower[h]
        + c[h][3] * roll(u[h], -1, 1)
        + c[h][4] * roll(u[h], 1, 1)
        for h in range(2)
    )


def presmooth(b, c):
    wb = c[0] * b
    u = sweep(wb, wb, c)
    return wb, u, (sweep(u, wb, c) - u) * c[5]


def kernel(
    n, wells,
    b_ref, s_ref, ax_ref, ay_ref, row_ref, col_ref, owner_ref, slot_ref, con_ref,
    out_ref, plan_ref,
    up0, dn0, below0, above0,
    ops1, below_ops1, above_ops1,
    b1, below_b1, above_b1,
    up_u, dn_u, below_u, above_u,
    m2, below_m2, above_m2,
    ops3, b3, all_ops, all_b, full,
    place, partial, got,
    near_send, near_recv, g_send, g_recv,
):
    me = lax.axis_index("tx")
    barrier = pltpu.get_barrier_semaphore()

    def greet(k, carry):
        pl.semaphore_signal(
            barrier, inc=1, device_id={"tx": lax.rem(me + k, n)}, device_id_type=pl.DeviceIdType.MESH
        )
        return carry

    lax.fori_loop(1, n, greet, 0)

    def near(slot, src_up, src_dn, dst_below, dst_above):
        up = pltpu.make_async_remote_copy(
            src_ref=src_up, dst_ref=dst_below, send_sem=near_send.at[slot, 0],
            recv_sem=near_recv.at[slot, 0], device_id={"tx": jnp.maximum(me - 1, 0)},
            device_id_type=pl.DeviceIdType.MESH,
        )
        dn = pltpu.make_async_remote_copy(
            src_ref=src_dn, dst_ref=dst_above, send_sem=near_send.at[slot, 1],
            recv_sem=near_recv.at[slot, 1], device_id={"tx": jnp.minimum(me + 1, n - 1)},
            device_id_type=pl.DeviceIdType.MESH,
        )

        def start():
            @pl.when(me > 0)
            def _():
                up.start()

            @pl.when(me < n - 1)
            def _():
                dn.start()

        def wait():
            @pl.when(me > 0)
            def _():
                up.wait_send()
                dn.wait_recv()

            @pl.when(me < n - 1)
            def _():
                dn.wait_send()
                up.wait_recv()

        return start, wait

    def gather(slot, source, dest):
        def copy(peer, index):
            return pltpu.make_async_remote_copy(
                src_ref=source(peer), dst_ref=dest.at[index], send_sem=g_send.at[slot, peer],
                recv_sem=g_recv.at[slot, index], device_id={"tx": peer},
                device_id_type=pl.DeviceIdType.MESH,
            )

        def start():
            def body(k, carry):
                copy(lax.rem(me + k, n), me).start()
                return carry

            lax.fori_loop(1, n, body, 0)

        def wait():
            def body(k, carry):
                peer = lax.rem(me + k, n)
                copy(peer, peer).wait_recv()
                copy(peer, peer).wait_send()
                return carry

            lax.fori_loop(1, n, body, 0)

        return start, wait

    def spread(w, carry):
        for k, ref in enumerate((row_ref, col_ref, slot_ref)):
            place[k, pl.ds(w, 1), :] = jnp.full((1, 128), ref[w], jnp.int32)
        return carry

    lax.fori_loop(0, wells, spread, 0, unroll=True)

    ny = b_ref.shape[1]
    pos = iota((8, ny), 0)
    b, s, ax, ay = b_ref[...], s_ref[...], ax_ref[...], ay_ref[...]

    s_last = s[8:] + jnp.where(pos == 6, roll(ax[8:], 1, 0), 0.0)
    send_up = jnp.zeros((8, ny), F32)
    send_dn = jnp.zeros((8, ny), F32)
    for k, (first, last) in enumerate(((s[:8], s_last), (ax[:8], ax[8:]), (ay[:8], ay[8:]), (b[:8], b[8:]))):
        here = pos // 2 == k
        send_up = jnp.where(here, roll(first, 2 * k, 0), send_up)
        send_dn = jnp.where(here, roll(last, 2 * k - 6, 0), send_dn)
    up0[...] = send_up
    dn0[...] = send_dn

    pl.semaphore_wait(barrier, n - 1)
    start0, wait0 = near(0, up0, dn0, below0, above0)
    start0()

    pairs = iota((8, 16), 1) // 2 == iota((8, 16), 0)
    odds = iota((8, 16), 1) == 2 * iota((8, 16), 0) + 1
    ops1[0] = rows_by(pairs, pair_cols(s))
    ops1[1] = rows_by(odds, pair_cols(ax))
    ops1[2] = rows_by(pairs, pair_cols(ay, True))
    start1, wait1 = near(1, ops1, ops1, below_ops1, above_ops1)
    start1()

    wait0()
    idx = iota((24, ny), 0)
    live = (idx < 18) | (idx >= 22)
    live &= ~((me == 0) & (idx >= 18))
    live &= ~((me == n - 1) & (idx >= 16) & (idx < 22))
    below, above = below0[...], above0[...]
    full0 = []
    for k, own in enumerate((s, ax, ay, b)):
        tail = jnp.where(pos < 2, roll(below, -2 * k, 0), roll(above, 6 - 2 * k, 0))
        whole0 = jnp.concatenate([own, tail], axis=0)
        full0.append(jnp.where(live, whole0, 1.0 if k == 0 else 0.0))
    c0 = coefficients(full0[0], full0[1], full0[2], live)
    wb0, u0, r0 = presmooth(full0[3], c0)

    b1[...] = rows_by(pairs, pair_cols(r0[:16]))
    start2, wait2 = near(2, b1, b1, below_b1, above_b1)
    start2()
    up_u[...] = u0[0:2]
    dn_u[...] = u0[14:16]
    start3, wait3 = near(3, up_u, dn_u, below_u, above_u)
    start3()

    wait1()
    n1 = ny // 2
    idx = iota((24, n1), 0)
    live = ~((me == 0) & (idx >= 16)) & ~((me == n - 1) & (idx >= 8) & (idx < 16))
    o1 = []
    for k in range(3):
        v = jnp.concatenate([ops1[k], below_ops1[k], above_ops1[k]], axis=0)
        o1.append(jnp.where(live, v, 1.0 if k == 0 else 0.0))
    c1 = coefficients(o1[0], o1[1], o1[2], live)

    out, inn = iota((16, 24), 0), iota((16, 24), 1)
    used = (out < 8) | (out >= 12)
    base = jnp.where(out < 8, 2 * out, 2 * out - 8)
    pairs2 = used & ((inn == base) | (inn == base + 1))
    odds2 = used & (inn == base + 1)
    n2 = ny // 4
    idx = iota((16, n2), 0)
    live2 = ((idx < 8) | (idx >= 12)) & ~((me == 0) & (idx >= 8)) & ~((me == n - 1) & (idx >= 4) & (idx < 12))
    o2 = [
        jnp.where(live2, rows_by(pairs2, pair_cols(o1[0])), 1.0),
        jnp.where(live2, rows_by(odds2, pair_cols(o1[1])), 0.0),
        jnp.where(live2, rows_by(pairs2, pair_cols(o1[2], True)), 0.0),
    ]
    out, inn = iota((8, 16), 0), iota((8, 16), 1)
    pairs3 = (out < 2) & (inn // 2 == out)
    odds3 = (out < 2) & (inn == 2 * out + 1)
    own3 = (
        rows_by(pairs3, pair_cols(o2[0])),
        rows_by(odds3, pair_cols(o2[1])),
        rows_by(pairs3, pair_cols(o2[2], True)),
    )
    for k in range(3):
        ops3[k] = own3[k][0:2]
        all_ops[me, k] = own3[k][0:2]
    start4, wait4 = gather(0, lambda peer: ops3, all_ops)
    start4()
    c2 = coefficients(o2[0], o2[1], o2[2], live2)

    wait2()
    b1e = jnp.where(live, jnp.concatenate([b1[...], below_b1[...], above_b1[...]], axis=0), 0.0)
    wb1, u1, r1 = presmooth(b1e, c1)
    b2 = rows_by(pairs2, pair_cols(r1))
    _, u2, r2 = presmooth(b2, c2)
    b3_own = rows_by(pairs3, pair_cols(r2))[0:2]
    b3[...] = b3_own
    all_b[me] = b3_own
    start5, wait5 = gather(1, lambda peer: b3, all_b)
    start5()
    m2[0] = u2[0:4]
    m2[1] = b2[0:4]
    start6, wait6 = near(4, m2, m2, below_m2, above_m2)
    start6()

    wait4()
    for k in range(3):
        for t in range(n):
            for h in range(2):
                full[k, h, t : t + 1, :] = all_ops[t, k, h : h + 1]
    s3, x3, y3 = ((full[k, 0], full[k, 1]) for k in range(3))
    c3 = coefficients_split(s3, x3, y3)
    s4 = pair_cols(s3[0] + s3[1])
    x4 = pair_cols(x3[1])
    y4 = pair_cols(y3[0] + y3[1], True)
    c4 = coefficients(s4, x4, y4, None, True)

    wait5()
    for t in range(n):
        for h in range(2):
            full[3, h, t : t + 1, :] = all_b[t, h : h + 1]
    wb3 = tuple(c3[h][0] * full[3, h] for h in range(2))
    u3 = sweep_split(wb3, wb3, c3)
    v3 = sweep_split(u3, wb3, c3)
    r3 = (v3[0] - u3[0]) * c3[0][5] + (v3[1] - u3[1]) * c3[1][5]
    wb4 = c4[0] * pair_cols(r3)
    u4 = lax.fori_loop(0, CSW - 1, lambda i, v: sweep(v, wb4, c4), wb4)
    e4 = twice_cols(u4)
    u3 = (u3[0] + e4, u3[1] + e4)
    u3 = sweep_split(sweep_split(u3, wb3, c3), wb3, c3)

    wait6()
    i, j = iota((16, n), 0), iota((16, n), 1)
    glob = 4 * me + jnp.where(i < 8, i, i - 16)
    held = (i < 8) | (i >= 12)
    e3 = rows_by(held & ((glob == 4 * j) | (glob == 4 * j + 1)), twice_cols(u3[0]))
    e3 += rows_by(held & ((glob == 4 * j + 2) | (glob == 4 * j + 3)), twice_cols(u3[1]))
    gap = jnp.zeros((4, n2), F32)
    u2e, b2e = (
        jnp.where(live2, jnp.concatenate([m2[k], below_m2[k], gap, above_m2[k]], axis=0), 0.0)
        for k in range(2)
    )
    wb2 = c2[0] * b2e
    u2 = sweep(sweep(u2e + e3, wb2, c2), wb2, c2)

    i, j = iota((24, 16), 0), iota((24, 16), 1)
    twice2 = j == jnp.where(i < 16, i // 2, i // 2 + 4)
    u1 = u1 + rows_by(twice2, twice_cols(u2))
    u1 = sweep(sweep(u1, wb1, c1), wb1, c1)

    wait3()
    i, j = iota((24, 24), 0), iota((24, 24), 1)
    twice1 = ((i < 18) & (j == i // 2)) | ((i >= 22) & (j == 23))
    bu, au = below_u[...], above_u[...]
    ends = jnp.concatenate([bu, jnp.zeros((4, ny), F32), au], axis=0)
    row24 = iota((24, ny), 0)
    live = (row24 < 18) | (row24 >= 22)
    live &= ~((me == 0) & (row24 >= 18))
    live &= ~((me == n - 1) & (row24 >= 16) & (row24 < 22))
    u0 = jnp.where(live, jnp.concatenate([u0[:16], ends], axis=0), 0.0)
    u0 = u0 + jnp.where(live, rows_by(twice1, twice_cols(u1)), 0.0)
    u0 = sweep(sweep(u0, wb0, c0), wb0, c0)[:16]
    out_ref[...] = u0

    picked = dot((place[0] == iota((wells, 128), 1)).astype(F32)[:, 0:16], u0)
    picked = jnp.concatenate([picked, jnp.zeros((wells, SCREEN), F32)], axis=1)
    col = place[1]
    chunk = ny // 256
    while chunk >= 1:
        width = 128 * (chunk + 1)
        there = jnp.concatenate([(col & (128 * chunk)) != 0] * (chunk + 1), axis=1)
        picked = jnp.where(there, picked[:, 128 * chunk : 128 * chunk + width], picked[:, :width])
        chunk //= 2
    moved = picked
    shift = jnp.concatenate([col, col], axis=1)
    for bit in (1, 2, 4, 8, 16, 32, 64):
        moved = jnp.where((shift & bit) != 0, roll(moved, -bit, 1), moved)
    terms = con_ref[...] * moved[:, :SCREEN]
    block = owner_ref[...] * BLK_DEV + place[2][:, 0:1]
    hot = block == iota((wells, n * BLK_DEV), 1)
    blocks = lax.dot_general(
        hot.astype(F32), terms, (((0,), (0,)), ((), ())), precision=lax.Precision.HIGHEST,
        preferred_element_type=F32,
    )
    partial[...] = blocks.reshape(n, BLK_DEV, SCREEN)
    start7, wait7 = gather(2, lambda peer: partial.at[peer], got)
    start7()
    got[me] = partial[me]
    wait7()
    plan_ref[...] = jnp.sum(got[...], axis=0)


def shards(n, misfit, storage, conduct_x, conduct_y, well_row, well_col, well_owner, well_slot, connection):
    rows, ny = misfit.shape
    wells = well_row.shape[0]
    vmem = pl.BlockSpec(memory_space=pltpu.VMEM)
    smem = pl.BlockSpec(memory_space=pltpu.SMEM)

    def buf(*shape):
        return pltpu.VMEM(shape, F32)

    n1, n2, n3 = ny // 2, ny // 4, ny // 8
    return pl.pallas_call(
        functools.partial(kernel, n, wells),
        out_shape=(
            jax.ShapeDtypeStruct((rows, ny), F32),
            jax.ShapeDtypeStruct((BLK_DEV, SCREEN), F32),
        ),
        in_specs=[vmem, vmem, vmem, vmem, smem, smem, vmem, smem, vmem],
        out_specs=(vmem, vmem),
        scratch_shapes=[
            buf(8, ny), buf(8, ny), buf(8, ny), buf(8, ny),
            buf(3, 8, n1), buf(3, 8, n1), buf(3, 8, n1),
            buf(8, n1), buf(8, n1), buf(8, n1),
            buf(2, ny), buf(2, ny), buf(2, ny), buf(2, ny),
            buf(2, 4, n2), buf(2, 4, n2), buf(2, 4, n2),
            buf(3, 2, n3), buf(2, n3), buf(n, 3, 2, n3), buf(n, 2, n3), buf(4, 2, n, n3),
            pltpu.VMEM((3, wells, 128), jnp.int32),
            buf(n, BLK_DEV, SCREEN), buf(n, BLK_DEV, SCREEN),
            pltpu.SemaphoreType.DMA((5, 2)), pltpu.SemaphoreType.DMA((5, 2)),
            pltpu.SemaphoreType.DMA((3, n)), pltpu.SemaphoreType.DMA((3, n)),
        ],
        compiler_params=pltpu.CompilerParams(
            collective_id=0, has_side_effects=True, vmem_limit_bytes=40 * 1024 * 1024
        ),
        name="vcycle",
    )(misfit, storage, conduct_x, conduct_y, well_row, well_col, well_owner, well_slot, connection)


def solution(mesh):
    tiles = P(("real", "tx"), None)
    return jax.shard_map(
        functools.partial(shards, mesh.shape["tx"]),
        mesh=mesh,
        in_specs=(tiles, tiles, tiles, tiles, P("tx"), P("tx"), P("tx", None), P("tx"), P("tx", None)),
        out_specs=(tiles, tiles),
        check_vma=False,
    )
```

time: 458 us -> 38.6 us (0.08)
  starting transfers between devices: 236 us -> 0 us
  local copies, waits for them, and re-layouts: 134 us -> 6.93 us
  blocking collectives: 40.6 us -> 0 us
  Pallas kernels: 0 us -> 30.8 us
  waiting for transfers between devices: 20.9 us -> 0 us
  other arithmetic: 19.5 us -> 0 us
    ppermute x73 -> x0, starting transfers between devices: 236 us -> none  [the longest x36 186 us: padded_2(): lax.ppermute(tail, axis, [(i, (i + 1) % count) for i in range(ends)])]
    gather x161 -> x0, local copies, waits for them, and re-layouts: 76.3 us -> none
    reshape x14 -> x0, local copies, waits for them, and re-layouts: 37.5 us -> none  [the longest x3 13.1 us: coarsen(): coarse_store = storage.reshape(rows // 2, 2, cols // 2, 2).sum(axis=(1, 3))]
    pallas_call x0 -> x1, Pallas kernels: none -> 30.8 us  [shards(): pl.pallas_call(functools.partial(kernel, n, wells), out_shape=(jax.ShapeD...]
    all_gather x1 -> x0, blocking collectives: 28.8 us -> none  [shards(): piece_terms = lax.all_gather(terms, 'tx', axis=0, tiled=True)]
    ppermute x73 -> x0, waiting for transfers between devices: 20.9 us -> none  [the longest x36 20.8 us: padded_2(): lax.ppermute(tail, axis, [(i, (i + 1) % count) for i in range(ends)])]
    reduce_sum x21 -> x0, other arithmetic: 13.9 us -> none  [the longest x8 5.79 us: coarsen(): coarse_store = storage.reshape(rows // 2, 2, cols // 2, 2).sum(axis=(1, 3))]
    unnamed x1 -> x0, blocking collectives: 11.8 us -> none
  transfers between devices with their start and end apart: 73 -> 0, of which waited for: 29 -> 0; matrix products, arithmetic and copies ran while one was open for 13% -> 0% of each run, Pallas kernels for 0% -> 0%
where the time goes in v1:
time: 38.6 us; the launch traced here: 38.4 us
  Pallas kernels  30.8 us (80%)
  local copies, waits for them, and re-layouts  6.93 us (18%)
  between operations  0.67 us (2%)
    pallas_call x1, Pallas kernels, shards(): pl.pallas_call(functools.partial(kernel, n, wells), out_shape=(jax.ShapeD...  30.8 us
    unnamed x19, local copies, waits for them, and re-layouts  6.93 us

profile of v1, /device:TPU:0, one launch (start us, length us, event | category | flops | bytes accessed | tf_op | source)
XLA Modules:
  0.0 38.4 jit_solution(1508596422236936189)
XLA Ops:
  0.6 0.0 copy-start.4
  0.6 0.0 copy-start.5
  0.7 0.8 %copy.11.owner_ref = s32[40,1]{1,0:T(8,128)S(1)} copy(s32[40,1]{0,1:T(1,128)} %param.15) | data formatting | bytes 320 | tf_op args[6]
  1.4 0.0 copy-done.4
  1.4 0.0 copy-done.5
  1.4 0.0 copy-start
  1.4 0.9 %copy-done = f32[16,2048]{1,0:T(8,128)S(1)} copy-done((f32[16,2048]{1,0:T(8,128)S(1)}, f32[16,2048]{1,0:T(8,128)}, u32[]{:S(2)}) %copy-start) | copy-done | bytes 131096
  2.3 0.0 copy-start.1
  2.3 0.9 %copy-done.1 = f32[16,2048]{1,0:T(8,128)S(1)} copy-done((f32[16,2048]{1,0:T(8,128)S(1)}, f32[16,2048]{1,0:T(8,128)}, u32[]{:S(2)}) %copy-start.1) | copy-done | bytes 131096
  3.2 0.0 copy-start.2
  3.2 0.9 %copy-done.2 = f32[16,2048]{1,0:T(8,128)S(1)} copy-done((f32[16,2048]{1,0:T(8,128)S(1)}, f32[16,2048]{1,0:T(8,128)}, u32[]{:S(2)}) %copy-start.2) | copy-done | bytes 131096
  4.1 0.0 copy-start.3
  4.1 0.9 %copy-done.3 = f32[16,2048]{1,0:T(8,128)S(1)} copy-done((f32[16,2048]{1,0:T(8,128)S(1)}, f32[16,2048]{1,0:T(8,128)}, u32[]{:S(2)}) %copy-start.3) | copy-done | bytes 131096
  5.0 0.0 copy-start.6
  5.0 0.7 %copy-done.6 = s32[40]{0:T(128)S(1)} copy-done((s32[40]{0:T(128)S(1)}, s32[40]{0:T(128)}, u32[]{:S(2)}) %copy-start.6) | copy-done | bytes 184
  5.7 0.0 copy-start.7
  5.7 0.7 %copy-done.7 = s32[40]{0:T(128)S(1)} copy-done((s32[40]{0:T(128)S(1)}, s32[40]{0:T(128)}, u32[]{:S(2)}) %copy-start.7) | copy-done | bytes 184
  6.3 30.8 %vcycle.1 = (f32[16,2048]{1,0:T(8,128)S(1)}, f32[8,128]{1,0:T(8,128)S(1)}) custom-call(f32[16,2048]{1,0:T(8,128)S(1)} %copy-done, f32[16,2048]{1,0:T(8,128)S(1)} %copy-done.1, f32[16,2048]{1,0:T(8,128)S(1)} %copy-done.2, f32[16,2048]{1,0:T(8,128)S(1)} %copy-done.3, s32[40]{0:T(128)S(1)} %copy-done.5, s32[40]{0:T(128)S(1)} %copy-done.6, ...), custom_call_target="tpu_custom_call" | custom-call | tf_op jit(solution)/shard_map/vcycle/pallas_call | solution.py:408
  37.1 0.7 %copy.14 = f32[16,2048]{1,0:T(8,128)} copy(f32[16,2048]{1,0:T(8,128)S(1)} %get-tuple-element.4) | data formatting | bytes 262144
  37.8 0.6 %copy.15 = f32[8,128]{1,0:T(8,128)} copy(f32[8,128]{1,0:T(8,128)S(1)} %get-tuple-element.5) | data formatting | bytes 8192
Async XLA Ops:
  0.6 0.8 %copy-start.4 = (f32[40,128]{1,0:T(8,128)S(1)}, f32[40,128]{1,0:T(8,128)}, u32[]{:S(2)}) copy-start(f32[40,128]{1,0:T(8,128)} %con_ref.1) | copy-start | bytes 61444
  0.6 0.8 %copy-start.5 = (s32[40]{0:T(128)S(1)}, s32[40]{0:T(128)}, u32[]{:S(2)}) copy-start(s32[40]{0:T(128)} %row_ref.1) | copy-start | bytes 484
  1.4 0.9 %copy-start = (f32[16,2048]{1,0:T(8,128)S(1)}, f32[16,2048]{1,0:T(8,128)}, u32[]{:S(2)}) copy-start(f32[16,2048]{1,0:T(8,128)} %b_ref.1) | copy-start | bytes 393220
  2.3 0.9 %copy-start.1 = (f32[16,2048]{1,0:T(8,128)S(1)}, f32[16,2048]{1,0:T(8,128)}, u32[]{:S(2)}) copy-start(f32[16,2048]{1,0:T(8,128)} %s_ref.1) | copy-start | bytes 393220
  3.2 0.9 %copy-start.2 = (f32[16,2048]{1,0:T(8,128)S(1)}, f32[16,2048]{1,0:T(8,128)}, u32[]{:S(2)}) copy-start(f32[16,2048]{1,0:T(8,128)} %ax_ref.1) | copy-start | bytes 393220
  4.1 0.9 %copy-start.3 = (f32[16,2048]{1,0:T(8,128)S(1)}, f32[16,2048]{1,0:T(8,128)}, u32[]{:S(2)}) copy-start(f32[16,2048]{1,0:T(8,128)} %ay_ref.1) | copy-start | bytes 393220
  5.0 0.7 %copy-start.6 = (s32[40]{0:T(128)S(1)}, s32[40]{0:T(128)}, u32[]{:S(2)}) copy-start(s32[40]{0:T(128)} %col_ref.1) | copy-start | bytes 484
  5.7 0.7 %copy-start.7 = (s32[40]{0:T(128)S(1)}, s32[40]{0:T(128)}, u32[]{:S(2)}) copy-start(s32[40]{0:T(128)} %slot_ref.1) | copy-start | bytes 484

commit v2 on v1

--- a/solution.py
+++ b/solution.py
@@ -24,6 +24,20 @@
     )
 
 
+def two_parts(x):
+    high = x.astype(jnp.bfloat16).astype(F32)
+    return jnp.concatenate([high, x - high], axis=0).astype(jnp.bfloat16)
+
+
+def short_dot(a, b):
+    return lax.dot_general(a, b, (((1,), (0,)), ((), ())), preferred_element_type=F32)
+
+
+def by_pick(x, pick):
+    y = short_dot(two_parts(x), pick.astype(F32).astype(jnp.bfloat16))
+    return y[: x.shape[0]] + y[x.shape[0] :]
+
+
 def roll(x, shift, axis):
     shift = shift % x.shape[axis]
     return x if shift == 0 else pltpu.roll(x, shift, axis)
@@ -35,7 +49,7 @@
     pick = (i == 2 * j + 1) if odd_only else (i // 2 == j)
     chunks = cols // 256
     stacked = jnp.concatenate([x[:, 256 * c : 256 * c + 256] for c in range(chunks)], axis=0)
-    y = dot(stacked, pick.astype(F32))
+    y = by_pick(stacked, pick)
     return jnp.concatenate([y[rows * c : rows * (c + 1)] for c in range(chunks)], axis=1)
 
 
@@ -44,12 +58,13 @@
     i, j = iota((128, 256), 0), iota((128, 256), 1)
     chunks = cols // 128
     stacked = jnp.concatenate([x[:, 128 * c : 128 * c + 128] for c in range(chunks)], axis=0)
-    y = dot(stacked, (j // 2 == i).astype(F32))
+    y = by_pick(stacked, j // 2 == i)
     return jnp.concatenate([y[rows * c : rows * (c + 1)] for c in range(chunks)], axis=1)
 
 
 def rows_by(pick, x):
-    return dot(pick.astype(F32), x)
+    pick = pick.astype(F32)
+    return short_dot(jnp.concatenate([pick, pick], axis=1).astype(jnp.bfloat16), two_parts(x))
 
 
 def coefficients(s, ax, ay, live, whole=False):
@@ -118,18 +133,26 @@
 
 def kernel(
     n, wells,
-    b_ref, s_ref, ax_ref, ay_ref, row_ref, col_ref, owner_ref, slot_ref, con_ref,
+    b_hbm, s_hbm, ax_hbm, ay_hbm, row_ref, col_ref, owner_ref, slot_ref, con_hbm,
     out_ref, plan_ref,
-    up0, dn0, below0, above0,
+    b_ref, s_ref, ax_ref, ay_ref, con_ref, up0, dn0, below0, above0,
     ops1, below_ops1, above_ops1,
     b1, below_b1, above_b1,
     up_u, dn_u, below_u, above_u,
     m2, below_m2, above_m2,
     ops3, b3, all_ops, all_b, full,
     place, partial, got,
-    near_send, near_recv, g_send, g_recv,
+    near_send, near_recv, g_send, g_recv, in_sem,
 ):
     me = lax.axis_index("tx")
+    loads = [
+        pltpu.make_async_copy(src, dst, in_sem.at[k])
+        for k, (src, dst) in enumerate(
+            ((s_hbm, s_ref), (ax_hbm, ax_ref), (ay_hbm, ay_ref), (b_hbm, b_ref), (con_hbm, con_ref))
+        )
+    ]
+    for load in loads:
+        load.start()
     barrier = pltpu.get_barrier_semaphore()
 
     def greet(k, carry):
@@ -201,7 +224,7 @@
         return start, wait
 
     def spread(w, carry):
-        for k, ref in enumerate((row_ref, col_ref, slot_ref)):
+        for k, ref in enumerate((row_ref, col_ref, slot_ref, owner_ref)):
             place[k, pl.ds(w, 1), :] = jnp.full((1, 128), ref[w], jnp.int32)
         return carry
 
@@ -209,6 +232,8 @@
 
     ny = b_ref.shape[1]
     pos = iota((8, ny), 0)
+    for load in loads[:4]:
+        load.wait()
     b, s, ax, ay = b_ref[...], s_ref[...], ax_ref[...], ay_ref[...]
 
     s_last = s[8:] + jnp.where(pos == 6, roll(ax[8:], 1, 0), 0.0)
@@ -380,8 +405,9 @@
     shift = jnp.concatenate([col, col], axis=1)
     for bit in (1, 2, 4, 8, 16, 32, 64):
         moved = jnp.where((shift & bit) != 0, roll(moved, -bit, 1), moved)
+    loads[4].wait()
     terms = con_ref[...] * moved[:, :SCREEN]
-    block = owner_ref[...] * BLK_DEV + place[2][:, 0:1]
+    block = (place[3] * BLK_DEV + place[2])[:, 0:1]
     hot = block == iota((wells, n * BLK_DEV), 1)
     blocks = lax.dot_general(
         hot.astype(F32), terms, (((0,), (0,)), ((), ())), precision=lax.Precision.HIGHEST,
@@ -399,6 +425,7 @@
     rows, ny = misfit.shape
     wells = well_row.shape[0]
     vmem = pl.BlockSpec(memory_space=pltpu.VMEM)
+    hbm = pl.BlockSpec(memory_space=pl.ANY)
     smem = pl.BlockSpec(memory_space=pltpu.SMEM)
 
     def buf(*shape):
@@ -411,25 +438,27 @@
             jax.ShapeDtypeStruct((rows, ny), F32),
             jax.ShapeDtypeStruct((BLK_DEV, SCREEN), F32),
         ),
-        in_specs=[vmem, vmem, vmem, vmem, smem, smem, vmem, smem, vmem],
+        in_specs=[hbm, hbm, hbm, hbm, smem, smem, smem, smem, hbm],
         out_specs=(vmem, vmem),
         scratch_shapes=[
+            buf(rows, ny), buf(rows, ny), buf(rows, ny), buf(rows, ny), buf(wells, SCREEN),
             buf(8, ny), buf(8, ny), buf(8, ny), buf(8, ny),
             buf(3, 8, n1), buf(3, 8, n1), buf(3, 8, n1),
             buf(8, n1), buf(8, n1), buf(8, n1),
             buf(2, ny), buf(2, ny), buf(2, ny), buf(2, ny),
             buf(2, 4, n2), buf(2, 4, n2), buf(2, 4, n2),
             buf(3, 2, n3), buf(2, n3), buf(n, 3, 2, n3), buf(n, 2, n3), buf(4, 2, n, n3),
-            pltpu.VMEM((3, wells, 128), jnp.int32),
+            pltpu.VMEM((4, wells, 128), jnp.int32),
             buf(n, BLK_DEV, SCREEN), buf(n, BLK_DEV, SCREEN),
             pltpu.SemaphoreType.DMA((5, 2)), pltpu.SemaphoreType.DMA((5, 2)),
             pltpu.SemaphoreType.DMA((3, n)), pltpu.SemaphoreType.DMA((3, n)),
+            pltpu.SemaphoreType.DMA((5,)),
         ],
         compiler_params=pltpu.CompilerParams(
-            collective_id=0, has_side_effects=True, vmem_limit_bytes=40 * 1024 * 1024
+            collective_id=0, has_side_effects=True, vmem_limit_bytes=56 * 1024 * 1024
         ),
         name="vcycle",
-    )(misfit, storage, conduct_x, conduct_y, well_row, well_col, well_owner, well_slot, connection)
+    )(misfit, storage, conduct_x, conduct_y, well_row, well_col, well_owner.reshape(wells), well_slot, connection)
 
 
 def solution(mesh):

time: 38.6 us -> 32 us (0.83)
  local copies, waits for them, and re-layouts: 6.93 us -> 2.17 us
  Pallas kernels: 30.8 us -> 29 us
    unnamed x19 -> x4, local copies, waits for them, and re-layouts: 6.93 us -> 2.17 us
    pallas_call x1, Pallas kernels: 30.8 us -> 29 us  [shards(): pl.pallas_call(functools.partial(kernel, n, wells), out_shape=(jax.ShapeD...]
where the time goes in v2:
time: 32 us; the launch traced here: 31.8 us
  Pallas kernels  29 us (91%)
  local copies, waits for them, and re-layouts  2.17 us (7%)
  between operations  0.65 us (2%)
    pallas_call x1, Pallas kernels, shards(): pl.pallas_call(functools.partial(kernel, n, wells), out_shape=(jax.ShapeD...  29 us
    unnamed x4, local copies, waits for them, and re-layouts  2.17 us

profile of v2, /device:TPU:0, one launch (start us, length us, event | category | flops | bytes accessed | tf_op | source)
XLA Modules:
  0.0 31.8 jit_solution(10331408152726081750)
XLA Ops:
  0.6 29.0 %vcycle.1 = (f32[16,2048]{1,0:T(8,128)}, f32[8,128]{1,0:T(8,128)}) custom-call(f32[16,2048]{1,0:T(8,128)} %b_hbm.1, f32[16,2048]{1,0:T(8,128)} %s_hbm.1, f32[16,2048]{1,0:T(8,128)} %ax_hbm.1, f32[16,2048]{1,0:T(8,128)} %ay_hbm.1, s32[40]{0:T(128)} %row_ref.1, s32[40]{0:T(128)} %col_ref.1, s32[40]{0:T(128)} %bitcast.1, s32[40]{0:T(128)} %slot_ref.1, ...), custom_call_target="tpu_custom_call" | custom-call | tf_op jit(solution)/shard_map/vcycle/pallas_call | solution.py:435
  29.6 0.0 copy-start
  29.7 1.6 %copy.13 = f32[16,2048]{1,0:T(8,128)} copy(f32[16,2048]{1,0:T(8,128)} %get-tuple-element.4) | data formatting | bytes 262144
  31.2 0.0 copy-done
  31.2 0.6 %copy.14 = f32[8,128]{1,0:T(8,128)} copy(f32[8,128]{1,0:T(8,128)S(1)} %copy-done) | data formatting | bytes 8192
Async XLA Ops:
  29.6 1.6 %copy-start = (f32[8,128]{1,0:T(8,128)S(1)}, f32[8,128]{1,0:T(8,128)}, u32[]{:S(2)}) copy-start(f32[8,128]{1,0:T(8,128)} %get-tuple-element.5) | copy-start | bytes 12292
